TPU v7x, 256 devices: a whole 4x4x8 slice. The times are simulated.
256 devices in a mesh: zero: 16 (over z_hi, y, core), seq: 16 (over x, z_lo).
Axes of the slice: x: 4, y: 4, z: 8 (z_hi: 2, z_lo: 4; z = z_hi * 4 + z_lo), core: 2. Of those that a mesh axis runs over, the one named last changes fastest.
Arguments:
- features: bfloat16 [16, 8192, 1536], P('zero', 'seq'), may hold values from -12 to 12, as said below
- lengths: int32 [16], replicated, may hold values from 512 to 8192, as said below
- kernel: bfloat16 [31, 1536], P(None, 'zero'), may hold values from -1 to 1
- gain: bfloat16 [1536], P('zero'), may hold values from 0.5 to 1.5
- bias: bfloat16 [1536], P('zero'), may hold values from -3 to 3
- projection: bfloat16 [1536, 1536], P('zero'), may hold values from -0.15625 to 0.15625
- cotangent: bfloat16 [16, 8192, 1536], P('zero', 'seq'), may hold values from -6 to 6
Outputs:
- layer_out: bfloat16 [16, 8192, 1536], P('zero', 'seq')
- grad_features: bfloat16 [16, 8192, 1536], P('zero', 'seq')
- grad_projection: bfloat16 [1536, 1536], P('zero')
- grad_kernel: bfloat16 [31, 1536], P(None, 'zero')
- grad_gain: float32 [1536], P('zero')
- grad_bias: float32 [1536], P('zero')
Inputs may be any that keep to these rules, and one draw needn't show every extreme that they name: `features`: input values; channels carry offsets that differ along the frames. `lengths`: at least one utterance has exactly 8192 valid frames.
All inputs are finite; a program needn't handle non-finite values.
Results may differ from a plain program's by a relative error of at most 0.0049.
Values may be sent and summed in bfloat16 or wider, within the bound.
A program may use at most 128 MiB of HBM per device.

v0:
```python
import jax
import jax.numpy as jnp
from jax import lax
from jax.sharding import PartitionSpec as P

EPS = 1e-05


def extended(cells, sides, width):
    for axis, dim in sides:
        count = lax.axis_size(axis)
        ends = count - 1
        head = lax.slice_in_dim(cells, 0, width, axis=dim)
        tail = lax.slice_in_dim(cells, cells.shape[dim] - width, cells.shape[dim], axis=dim)
        cells = jnp.concatenate(
            [
                lax.ppermute(tail, axis, [(i, (i + 1) % count) for i in range(ends)]),
                cells,
                lax.ppermute(head, axis, [((i + 1) % count, i) for i in range(ends)]),
            ],
            axis=dim,
        )
    return cells


def shards(features, lengths, kernel, gain, bias, projection, cotangent):
    frames = features.shape[1]
    width = features.shape[2]
    member = lax.axis_index("zero")
    positions = lax.axis_index("seq") * frames + jnp.arange(frames, dtype=jnp.int32)
    own_length = jnp.sum(
        jnp.where(jnp.arange(lengths.shape[0], dtype=jnp.int32) == member, lengths, 0)
    )
    keep = (positions < own_length).astype(jnp.float32)[:, None]
    count = jnp.sum(lengths).astype(jnp.float32)
    small = jnp.concatenate([kernel, gain[None, :], bias[None, :]], axis=0)
    full_proj, full_small = (
        lax.all_gather(projection, "zero", axis=0, tiled=True),
        lax.all_gather(small, "zero", axis=1, tiled=True),
    )
    taps = full_small[:-2].astype(jnp.float32)
    scale_g = full_small[-2].astype(jnp.float32)
    shift_b = full_small[-1].astype(jnp.float32)
    ntaps = taps.shape[0]
    reach = ntaps // 2
    inputs = features[0] * keep.astype(jnp.bfloat16)
    padded = extended(inputs, (("seq", 0),), reach).astype(jnp.float32)
    conv = jnp.zeros((frames, width), jnp.float32)
    for shift in range(ntaps):
        conv = conv + taps[shift][None, :] * padded[shift : shift + frames]
    mean = lax.psum(jnp.sum(conv * keep, axis=0), ("zero", "seq")) / count
    deviation = (conv - mean) * keep
    var = lax.psum(jnp.sum(deviation * deviation, axis=0), ("zero", "seq")) / count
    rstd = lax.rsqrt(var + EPS)
    normed = (conv - mean) * rstd
    pre = normed * scale_g + shift_b
    sig = jax.nn.sigmoid(pre)
    hidden = (keep * pre * sig).astype(jnp.bfloat16)
    output = jnp.dot(hidden, full_proj, preferred_element_type=jnp.float32).astype(jnp.bfloat16)
    upstream = cotangent[0]
    back = lax.dot_general(
        upstream, full_proj, (((1,), (1,)), ((), ())), preferred_element_type=jnp.float32
    )
    dpre = keep * back * (sig * (1.0 + pre * (1.0 - sig)))
    bias_sum, gain_sum = lax.psum(
        (jnp.sum(dpre, axis=0), jnp.sum(dpre * normed, axis=0)), ("zero", "seq")
    )
    dconv = keep * rstd * scale_g * (dpre - bias_sum / count - normed * gain_sum / count)
    dpad = extended(dconv, (("seq", 0),), reach)
    dframes = jnp.zeros((frames, width), jnp.float32)
    rows = []
    for shift in range(ntaps):
        dframes = (
            dframes + taps[shift][None, :] * dpad[2 * reach - shift : 2 * reach - shift + frames]
        )
        rows.append(jnp.sum(dconv * padded[shift : shift + frames], axis=0))
    grad_features = (keep * dframes).astype(jnp.bfloat16)[None]
    kernel_term = jnp.stack(rows, axis=0)
    root = lax.rsqrt(count)
    weight_term = lax.dot_general(
        hidden, upstream, (((0,), (0,)), ((), ())), preferred_element_type=jnp.float32
    )
    weight_part, kernel_part = (
        lax.psum_scatter(weight_term, "zero", scatter_dimension=0, tiled=True),
        lax.psum_scatter(kernel_term, "zero", scatter_dimension=1, tiled=True),
    )
    weight_total, kernel_total = lax.psum((weight_part, kernel_part), "seq")
    grad_projection = (weight_total * root).astype(jnp.bfloat16)
    grad_kernel = (kernel_total * root).astype(jnp.bfloat16)
    share = width // lax.axis_size("zero")
    offset = member * share
    grad_gain = lax.dynamic_slice_in_dim(gain_sum * root, offset, share)
    grad_bias = lax.dynamic_slice_in_dim(bias_sum * root, offset, share)
    return (output[None], grad_features, grad_projection, grad_kernel, grad_gain, grad_bias)


def solution(mesh):
    in_specs = (
        P("zero", "seq", None),
        P(),
        P(None, "zero"),
        P("zero"),
        P("zero"),
        P("zero", None),
        P("zero", "seq", None),
    )
    out_specs = (
        P("zero", "seq", None),
        P("zero", "seq", None),
        P("zero", None),
        P(None, "zero"),
        P("zero"),
        P("zero"),
    )
    return jax.shard_map(shards, mesh=mesh, in_specs=in_specs, out_specs=out_specs, check_vma=False)
```

profile of v0, /device:TPU:1, one launch (start us, length us, event | category | flops | bytes accessed | tf_op | source)
XLA Modules:
  0.0 621.9 jit_solution(15073389660230220618)
XLA Ops:
  7.3 0.7 all-gather.3.cloned.1.call-update
  8.0 1.3 fusion.102
  9.3 0.6 fusion.100
  10.0 1.6 bitcast_multiply_fusion
  11.5 0.6 fusion.104
  12.2 4.4 collective-permute-start
  16.5 1.3 collective-permute-start.1
  17.9 34.1 %all-gather = bf16[16,96,33]{1,2,0:T(8,128)(2,1)S(1)} all-gather(bf16[1,96,33]{1,2,0:T(8,128)(2,1)S(1)} %maximum_bitcast_fusion), channel_id=1, replica_groups=mesh['zero'=16,'seq'=16] {'zero'}, dimensions={0}, use_global_device_ids=true | all-gather | bytes 107712 | tf_op jit(solution)/shard_map/all_gather | solution.py:39
  52.2 0.6 fusion.97
  53.4 0.7 fusion.98
  54.7 0.5 maximum_convert_fusion
  55.2 13.5 %multiply_reduce_fusion.33 = (f32[1536]{0:T(1024)S(1)}, f32[512,1536]{1,0:T(8,128)}) fusion(f32[512]{0:T(512)S(1)} %fusion.98, f32[542,1536]{1,0:T(8,128)S(1)} %maximum_convert_fusion, f32[1536]{0:T(1024)S(1)} %get-tuple-element.40, f32[1536]{0:T(1024)S(1)} %get-tuple-element.41, f32[1536]{0:T(1024)S(1)} %get-tuple-element.42, ...), kind=kLoop, calls=%fused_computation.182 | loop fusion | flops 49543680 | bytes 100861952 | tf_op jit(solution)/shard_map/reduce_sum | solution.py:51
  68.7 78.8 %psum.42 = f32[1536]{0:T(1024)S(1)} all-reduce(f32[1536]{0:T(1024)S(1)} %get-tuple-element.77), channel_id=1, replica_groups=mesh['zero'=16,'seq'=16] {'zero','seq'}, use_global_device_ids=true, to_apply=%region_2.3 | all-reduce | flops 1536 | bytes 12288 | tf_op jit(solution)/shard_map/psum | solution.py:51
  147.5 2.4 multiply_reduce_fusion.32
  149.9 74.3 %psum.43 = f32[1536]{0:T(1024)S(1)} all-reduce(f32[1536]{0:T(1024)S(1)} %multiply_reduce_fusion.32), channel_id=1, replica_groups=mesh['zero'=16,'seq'=16] {'zero','seq'}, use_global_device_ids=true, to_apply=%region_5.6 | all-reduce | flops 1536 | bytes 12288 | tf_op jit(solution)/shard_map/psum | solution.py:53
  224.2 8.6 %fusion.92 = f32[1536,1536]{1,0:T(8,128)} fusion(bf16[1,512,1536]{2,1,0:T(8,128)(2,1)S(1)} %copy-done, f32[512,1536]{1,0:T(8,128)} %get-tuple-element.78, f32[1536]{0:T(1024)S(1)} %copy-done.5, f32[1536]{0:T(1024)S(1)} %copy-done.4, f32[1536]{0:T(1024)S(1)} %add_rsqrt_fusion, f32[1536]{0:T(1024)S(1)} %broadcast_divide_fusion.1, f32[512]{0:T(512)S(1)} %fusion.98), kind=kOutput, calls=%fused_computation.188 | convolution fusion | flops 2423783424 | bytes 14182400 | tf_op jit(solution)/shard_map/dot_general | solution.py:80
  233.0 7.7 %fusion.101 = (f32[1536]{0:T(1024)S(1)}, f32[1536]{0:T(1024)S(1)}, f32[512,1536]{1,0:T(8,128)}) fusion(f32[1536]{0:T(1024)S(1)} %add_rsqrt_fusion, f32[512,1536]{1,0:T(8,128)} %get-tuple-element.78, f32[1536]{0:T(1024)S(1)} %broadcast_divide_fusion.1, f32[1536]{0:T(1024)S(1)} %copy-done.5, f32[1536]{0:T(1024)S(1)} %copy-done.4, ...), kind=kOutput, calls=%fused_computation.242 | convolution fusion | flops 2428498944 | bytes 12621824 | tf_op jit(solution)/shard_map/dot_general | solution.py:61
  240.8 107.4 %all-reduce = (f32[1536]{0:T(1024)S(1)}, f32[1536]{0:T(1024)S(1)}) all-reduce(f32[1536]{0:T(1024)S(1)} %get-tuple-element.38, f32[1536]{0:T(1024)S(1)} %get-tuple-element.37), channel_id=1, replica_groups=mesh['zero'=16,'seq'=16] {'zero','seq'}, use_global_device_ids=true, to_apply=%region_9.10 | all-reduce | flops 3072 | bytes 24576 | tf_op jit(solution)/shard_map/psum | solution.py:65
  348.2 27.9 %multiply_reduce_fusion = (f32[1536]{0:T(1024)S(1)}, f32[1536]{0:T(1024)S(1)}, f32[1536]{0:T(1024)S(1)}, f32[1536]{0:T(1024)S(1)}, f32[1536]{0:T(1024)S(1)}, /*i...) fusion(f32[542,1536]{1,0:T(8,128)} %copy-done.1, ...), kind=kLoop, calls=%fused_computation.145 | loop fusion | flops 35361792 | bytes 66203652 | tf_op jit(solution)/shard_map/reduce_sum | solution.py:76
  376.1 5.1 multiply_reduce_fusion.1
  381.7 1.3 collective-permute-start.2
  383.0 4.0 collective-permute-start.3
  387.3 1.2 copy.15
  388.6 7.4 %fusion.91 = bf16[1,512,1536]{2,1,0:T(8,128)(2,1)} fusion(bf16[1536,1536]{1,0:T(8,128)(2,1)} %all-gather.3.cloned.1.call-done, f32[512,1536]{1,0:T(8,128)} %get-tuple-element.78, f32[1536]{0:T(1024)S(1)} %copy-done.5, f32[1536]{0:T(1024)S(1)} %copy-done.4, f32[1536]{0:T(1024)S(1)} %add_rsqrt_fusion, f32[1536]{0:T(1024)S(1)} %broadcast_divide_fusion.1, ...), kind=kOutput, calls=%fused_computation.186 | convolution fusion | flops 2424569856 | bytes 9463808 | tf_op jit(solution)/shard_map/dot_general | solution.py:59
  395.9 0.6 dynamic-slice_multiply_fusion
  396.6 51.0 %fusion.95 = bf16[1,512,1536]{2,1,0:T(8,128)(2,1)} fusion(f32[512,1536]{1,0:T(8,128)} %copy-done.3, f32[15,1536]{1,0:T(8,128)S(1)} %collective-permute-done.3, f32[1536]{0:T(1024)S(1)} %get-tuple-element.40, f32[1536]{0:T(1024)S(1)} %get-tuple-element.41, f32[1536]{0:T(1024)S(1)} %get-tuple-element.42, f32[1536]{0:T(1024)S(1)} %get-tuple-element.43, ...), kind=kLoop, calls=%fused_computation.192 | loop fusion | flops 73138176 | bytes 5095424 | tf_op jit(solution)/shard_map/broadcast_in_dim | solution.py:77
  447.6 13.7 %reduce-scatter.7.cloned.1.call-done = f32[96,31]{1,0:T(8,128)} async-done(((f32[1536,31]{1,0:T(8,128)}), f32[96,31]{1,0:T(8,128)}) %reduce-scatter.7.cloned.1.call-update) | async-done | bytes 11920
  461.3 0.9 copy.16
  462.2 65.5 %psum.47 = f32[31,96]{1,0:T(8,128)S(1)} all-reduce(f32[31,96]{1,0:T(8,128)S(1)} %copy.16), channel_id=1, replica_groups=mesh['zero'=16,'seq'=16] {'seq'}, use_global_device_ids=true, to_apply=%region_44.45 | all-reduce | flops 2976 | bytes 23808 | tf_op jit(solution)/shard_map/psum | solution.py:87
  527.7 0.6 multiply_convert_fusion.2
  528.3 85.3 %all-reduce.3.cloned.1.call-done = f32[96,1536]{1,0:T(8,128)} async-done(((f32[96,1536]{1,0:T(8,128)}), f32[96,1536]{1,0:T(8,128)}) %all-reduce.3.cloned.1.call-update) | async-done | bytes 589840 | tf_op jit(solution)/shard_map/psum | solution.py:87
  613.5 1.8 multiply_convert_fusion.1
  (73 shorter events, 1.6 us)
Async XLA Ops:
  7.2 217.0 %copy-start = (bf16[1,512,1536]{2,1,0:T(8,128)(2,1)S(1)}, bf16[1,512,1536]{2,1,0:T(8,128)(2,1)}, u32[]{:S(2)}) copy-start(bf16[1,512,1536]{2,1,0:T(8,128)(2,1)} %param.13) | copy-start | bytes 4718596
  7.2 10.7 %copy-start.7 = (bf16[96]{0:T(256)(128)(2,1)S(1)}, bf16[96]{0:T(256)(128)(2,1)}, u32[]{:S(2)}) copy-start(bf16[96]{0:T(256)(128)(2,1)} %param.11) | copy-start | bytes 580
  7.2 10.7 %copy-start.8 = (bf16[96]{0:T(256)(128)(2,1)S(1)}, bf16[96]{0:T(256)(128)(2,1)}, u32[]{:S(2)}) copy-start(bf16[96]{0:T(256)(128)(2,1)} %param.10) | copy-start | bytes 580
  7.2 10.7 %copy-start.6 = (bf16[31,96]{1,0:T(8,128)(2,1)S(1)}, bf16[31,96]{1,0:T(8,128)(2,1)}, u32[]{:S(2)}) copy-start(bf16[31,96]{1,0:T(8,128)(2,1)} %param.9) | copy-start | bytes 17860
  7.2 225.8 %all-gather.3.cloned.1.call-start = ((), (), s32[]{:S(2)}) async-start(), calls=%async_computation.2 | async-start | bytes 5013504 | tf_op jit(solution)/shard_map/all_gather | solution.py:38
  7.9 388.6 %reduce-scatter.5.cloned.1.call-start = ((), (), s32[]{:S(2)}) async-start(), calls=%async_computation.3 | async-start | bytes 10027008 | tf_op jit(solution)/shard_map/reduce_scatter | solution.py:84
  12.2 42.5 %collective-permute-start = (bf16[15,1536]{1,0:T(8,128)(2,1)}, bf16[15,1536]{1,0:T(8,128)(2,1)S(1)}, u32[]{:S(2)}, u32[]{:S(2)}) collective-permute-start(bf16[15,1536]{1,0:T(8,128)(2,1)} %get-tuple-element.81), channel_id=1, source_target_pairs={{0,1},{1,2},{2,3},{3,4},{4,5},{5,6},{6,7},{7,8},{8,9},{9,10},{10,1... | collective-permute-start | bytes 138248 | tf_op jit(solution)/shard_map/ppermute | solution.py:17
  16.5 38.1 %collective-permute-start.1 = (bf16[15,1536]{1,0:T(8,128)(2,1)S(1)}, bf16[15,1536]{1,0:T(8,128)(2,1)S(1)}, u32[]{:S(2)}, u32[]{:S(2)}) collective-permute-start(bf16[15,1536]{1,0:T(8,128)(2,1)S(1)} %get-tuple-element.82), channel_id=1, source_target_pairs={{1,0},{2,1},{3,2},{4,3},{5,4},{6,5},{7,6},{8,7},{9,8},{10,9},{11,1... | collective-permute-start | bytes 138248 | tf_op jit(solution)/shard_map/ppermute | solution.py:19
  55.2 13.5 %copy-start.1 = (f32[542,1536]{1,0:T(8,128)}, f32[542,1536]{1,0:T(8,128)S(1)}, u32[]{:S(2)}) copy-start(f32[542,1536]{1,0:T(8,128)S(1)} %maximum_convert_fusion) | copy-start | bytes 9990148
  68.7 155.5 %copy-start.4 = (f32[1536]{0:T(1024)S(1)}, f32[1536]{0:T(1024)}, u32[]{:S(2)}) copy-start(f32[1536]{0:T(1024)} %get-tuple-element.70) | copy-start | bytes 18436
  68.7 155.6 %copy-start.5 = (f32[1536]{0:T(1024)S(1)}, f32[1536]{0:T(1024)}, u32[]{:S(2)}) copy-start(f32[1536]{0:T(1024)} %get-tuple-element.71) | copy-start | bytes 18436
  232.9 228.4 %reduce-scatter.7.cloned.1.call-start = ((), (), s32[]{:S(2)}) async-start(), calls=%async_computation.5 | async-start | bytes 835584
  348.2 28.0 %copy-start.2 = (f32[542,1536]{1,0:T(8,128)S(1)}, f32[542,1536]{1,0:T(8,128)}, u32[]{:S(2)}) copy-start(f32[542,1536]{1,0:T(8,128)} %copy-done.1) | copy-start | bytes 9990148
  376.1 5.6 copy-start.3
  381.7 14.9 %collective-permute-start.2 = (f32[15,1536]{1,0:T(8,128)S(1)}, f32[15,1536]{1,0:T(8,128)S(1)}, u32[]{:S(2)}, u32[]{:S(2)}) collective-permute-start(f32[15,1536]{1,0:T(8,128)S(1)} %get-tuple-element.79), channel_id=1, source_target_pairs={{1,0},{2,1},{3,2},{4,3},{5,4},{6,5},{7,6},{8,7},{9,8},{10,9},{11,1... | collective-permute-start | bytes 276488 | tf_op jit(solution)/shard_map/ppermute | solution.py:19
  383.0 13.6 %collective-permute-start.3 = (f32[15,1536]{1,0:T(8,128)S(1)}, f32[15,1536]{1,0:T(8,128)S(1)}, u32[]{:S(2)}, u32[]{:S(2)}) collective-permute-start(f32[15,1536]{1,0:T(8,128)S(1)} %get-tuple-element.80), channel_id=1, source_target_pairs={{0,1},{1,2},{2,3},{3,4},{4,5},{5,6},{6,7},{7,8},{8,9},{9,10},{10,1... | collective-permute-start | bytes 276488 | tf_op jit(solution)/shard_map/ppermute | solution.py:17
  388.5 225.0 %all-reduce.3.cloned.1.call-start = ((), (), s32[]{:S(2)}) async-start(), calls=%async_computation.4 | async-start | bytes 1179648 | tf_op jit(solution)/shard_map/psum | solution.py:87
Sparse Core Ops, SparseCore 0:
  10.8 85.6 all-gather.2
  233.0 145.3 reduce-scatter.4
  388.6 72.6 reduce-scatter.6
  463.8 149.6 all-reduce.2
where the time goes:
time: 633 us; the launch traced here: 622 us
  blocking collectives  360 us (57%)
  other arithmetic  108 us (17%)
  waiting for transfers between devices  99.7 us (16%)
  matrix products  23.8 us (4%)
  between operations  15 us (2%)
  starting transfers between devices  11.1 us (2%)
    psum x1, blocking collectives, shards(): lax.psum((jnp.sum(dpre, axis=0), jnp.sum(dpre * normed, axis=0)), ('zero'...  107 us
    psum x1, waiting for transfers between devices, shards(): weight_total, kernel_total = lax.psum((weight_part, kernel_part), 'seq')  85.3 us
    psum x1, blocking collectives, shards(): mean = lax.psum(jnp.sum(conv * keep, axis=0), ('zero', 'seq')) / count  78.8 us
    psum x1, blocking collectives, shards(): lax.psum(jnp.sum(deviation * deviation, axis=0), ('zero', 'seq')) / count  74.3 us
    psum x1, blocking collectives, shards(): weight_total, kernel_total = lax.psum((weight_part, kernel_part), 'seq')  65.5 us
    broadcast_in_dim x1, other arithmetic, shards(): grad_features = (keep * dframes).astype(jnp.bfloat16)[None]  51 us
    all_gather x1, blocking collectives, shards(): lax.all_gather(small, 'zero', axis=1, tiled=True)  34.1 us
    reduce_sum x2, other arithmetic, shards(): rows.append(jnp.sum(dconv * padded[shift:shift + frames], axis=0))  33 us
  transfers between devices with their start and end apart: 8, of which 2 were waited for; matrix products, arithmetic and copies ran while one was open for 22% of the time, Pallas kernels for 0%

commit v1 on v0

v1 whole, which is shorter than its diff:
```python
import functools

import jax
import jax.numpy as jnp
from jax import lax
from jax.experimental import pallas as pl
from jax.experimental.pallas import tpu as pltpu
from jax.sharding import PartitionSpec as P

EPS = 1e-05
LANES = 128
HALO = 16
MESH = pl.DeviceIdType.MESH
F32 = jnp.float32
BF16 = jnp.bfloat16


class Dims:
    def __init__(self, zero, seq, frames, width, taps):
        self.nc = 2
        self.nzh = 2
        self.ny = zero // 4
        self.nx = 2 if seq == 4 else 4
        self.nzl = seq // self.nx
        self.zero, self.seq = zero, seq
        self.f, self.d, self.k = frames, width, taps
        self.nt = width // LANES
        self.blk = width // zero
        self.ext = frames + 2 * HALO
        self.chunk = min(128, frames)
        self.q = self.ny * self.nzh
        self.half = self.blk // 2
        self.cols = width // self.nx
        self.piece = self.blk // self.nzl
        self.pad_piece = -(-self.piece // 16) * 16
        self.sub = self.nzl // 2
        self.win = 4 * self.blk // LANES
        self.krows = -(-(taps + 2) // 8) * 8
        self.srows = -(-(taps + 2) // 16) * 16


def fold(values):
    rows = values.shape[0]
    return jnp.sum(values.reshape(rows // 8, 8, LANES), axis=0)


def kernel(
    g, sc, feat, cot, proj, small, keep,
    out, gfeat, gproj, gsmall,
    x_s, cv, dp, tap, full, hid, hid_t, ht2, cot_sib, halo, sm,
    a1, b1, a2, b2, st1, st2, gacc, gfull, gsend, ga, gb,
    wf, ws, r1x, r1y, s0, s1, r2x, r2y, tt, r3, wfin, asm,
    ssem, rsem, halo_s, halo_r, hal2_s, hal2_r, cot_s, cot_r, pj_s, pj_r, ht_s, ht_r,
    p1_s, p1_r, p2_s, p2_r, p3_s, p3_r,
):
    zi = lax.axis_index("zero")
    si = lax.axis_index("seq")
    c = zi % g.nc
    y = (zi // g.nc) % g.ny
    zh = zi // (g.nc * g.ny)
    zl = si % g.nzl
    x = si // g.nzl

    def zero_of(h, yy, cc):
        return (h * g.ny + yy) * g.nc + cc

    def seq_of(xx, zz):
        return xx * g.nzl + zz

    sibling = (zero_of(zh, y, 1 - c), si)

    def remote(src, dst, ss, rs, device):
        return pltpu.make_async_remote_copy(
            src_ref=src, dst_ref=dst, send_sem=ss, recv_sem=rs,
            device_id=device, device_id_type=MESH,
        )

    def in_zero(peer):
        return (peer, si)

    def in_seq(peer):
        return (zi, peer)

    def spread(buf, e, me, n, dev):
        @pl.loop(1, n)
        def _(o):
            peer = (me + o) % n
            remote(buf.at[me], buf.at[me], ssem.at[e, o], rsem.at[e, me], dev(peer)).start()

    def gathered(buf, e, me, n, dev):
        @pl.loop(1, n)
        def _(o):
            peer = (me + n - o) % n
            remote(buf.at[peer], buf.at[peer], ssem.at[e, o], rsem.at[e, peer], dev(peer)).wait()

    barrier = pltpu.get_barrier_semaphore()

    @pl.loop(1, g.zero)
    def _(o):
        pl.semaphore_signal(barrier, inc=1, device_id=((zi + o) % g.zero, si), device_id_type=MESH)

    @pl.loop(1, g.seq)
    def _(o):
        pl.semaphore_signal(barrier, inc=1, device_id=(zi, (si + o) % g.seq), device_id_type=MESH)

    @pl.loop(1, g.nzl)
    def _(o):
        pl.semaphore_signal(
            barrier, inc=1,
            device_id=(zero_of(1 - zh, y, c), seq_of(x, (zl + o) % g.nzl)), device_id_type=MESH,
        )

    @pl.loop(0, g.nt)
    def _(l):
        lane = pl.ds(pl.multiple_of(l * LANES, LANES), LANES)
        x_s[l, HALO:HALO + g.f, :] = feat[:, lane].astype(F32) * keep[HALO:HALO + g.f, :]

    own_rows = pl.ds(pl.multiple_of(zi * g.blk, 16), g.blk)
    full[own_rows, :] = proj[...]
    sm[zi] = small[...]
    pl.semaphore_wait(barrier, g.zero - 1 + g.seq - 1 + g.nzl - 1)

    spread(sm, 0, zi, g.zero, in_zero)
    right = in_seq((si + 1) % g.seq)
    left = in_seq((si + g.seq - 1) % g.seq)
    halo_right = remote(feat.at[pl.ds(g.f - HALO, HALO)], halo.at[0], halo_s.at[0], halo_r.at[0], right)
    halo_left = remote(feat.at[pl.ds(0, HALO)], halo.at[1], halo_s.at[1], halo_r.at[1], left)
    halo_right.start()
    halo_left.start()

    def block(index):
        return full.at[pl.ds(pl.multiple_of(index * g.blk, 16), g.blk)]

    def send_block(index, slot, device):
        remote(block(index), block(index), pj_s.at[slot], pj_r.at[index], device).start()

    def wait_block(index):
        remote(block(index), block(index), pj_s.at[0], pj_r.at[index], sibling).wait_recv()

    other = zero_of(1 - zh, y, c)
    mirror = (other, seq_of(x, g.nzl - 1 - zl))
    send_block(zi, 0, mirror)

    @pl.loop(1, g.ny)
    def _(o):
        send_block(zi, o, in_zero(zero_of(zh, (y + o) % g.ny, c)))

    cot_copy = remote(cot, cot_sib, cot_s, cot_r, sibling)
    send_block(zi, g.ny, sibling)
    cot_copy.start()

    gathered(sm, 0, zi, g.zero, in_zero)
    for w in range(g.zero // 4):
        total = None
        for i in range(4):
            row = lax.broadcasted_iota(jnp.int32, (LANES, 4 * g.blk), 0)
            col = lax.broadcasted_iota(jnp.int32, (LANES, 4 * g.blk), 1)
            place = jnp.where((col == row + i * g.blk) & (row < g.blk), 1.0, 0.0).astype(BF16)
            term = jnp.dot(sm[4 * w + i], place, preferred_element_type=F32)
            total = term if total is None else total + term
        for j in range(g.win):
            tap[g.win * w + j] = total[:, j * LANES:(j + 1) * LANES]
    halo_right.wait()
    halo_left.wait()

    @pl.loop(0, g.nt)
    def _(l):
        lane = pl.ds(pl.multiple_of(l * LANES, LANES), LANES)
        x_s[l, 0:HALO, :] = halo[0, :, lane].astype(F32) * keep[0:HALO, :]
        x_s[l, HALO + g.f:, :] = halo[1, :, lane].astype(F32) * keep[HALO + g.f:, :]

    own_keep = keep.at[pl.ds(HALO, g.f)]

    def conv_tiles(first, last):
        @pl.loop(first, last)
        def _(l):
            acc = jnp.zeros((g.f, LANES), F32)
            for k in range(g.k):
                acc = acc + tap[l, k:k + 1, :] * x_s[l, k + 1:k + 1 + g.f, :]
            cv[l, HALO:HALO + g.f, :] = acc
            mask = own_keep[...]
            mean = jnp.sum(fold(acc * mask), axis=0, keepdims=True) * sc[32]
            dev = (cv[l, HALO:HALO + g.f, :] - mean) * mask
            a1[zi, pl.ds(l, 1), :] = mean
            a1[zi, pl.ds(g.nt + l, 1), :] = jnp.sum(fold(dev * dev), axis=0, keepdims=True)

    def pooled(buf, n, base, inverse):
        total = None
        for i in range(n):
            term = sc[base + i] * buf[i, 0:g.nt, :]
            total = term if total is None else total + term
        mean = total * inverse
        squares = None
        for i in range(n):
            dev = buf[i, 0:g.nt, :] - mean
            term = buf[i, g.nt:2 * g.nt, :] + sc[base + i] * (dev * dev)
            squares = term if squares is None else squares + term
        return mean, squares

    conv_tiles(0, g.nt // 2)
    wait_block(other)
    send_block(other, g.ny + 1, sibling)

    @pl.loop(1, g.ny)
    def _(o):
        send_block(other, g.ny + 1 + o, in_zero(zero_of(zh, (y + o) % g.ny, c)))

    @pl.loop(1, g.ny)
    def _(o):
        index = zero_of(zh, (y + o) % g.ny, c)
        wait_block(index)
        send_block(index, 2 * g.ny + o, sibling)

    conv_tiles(g.nt // 2, g.nt)
    spread(a1, 1, zi, g.zero, in_zero)
    gathered(a1, 1, zi, g.zero, in_zero)
    mean_a, squares_a = pooled(a1, g.zero, 0, sc[33])
    b1[si, 0:g.nt, :] = mean_a
    b1[si, g.nt:2 * g.nt, :] = squares_a
    spread(b1, 2, si, g.seq, in_seq)

    @pl.loop(1, g.ny)
    def _(o):
        index = zero_of(1 - zh, (y + o) % g.ny, c)
        wait_block(index)
        send_block(index, 3 * g.ny - 1 + o, sibling)

    @pl.loop(0, g.nzh * g.ny)
    def _(j):
        wait_block(j * g.nc + 1 - c)

    @pl.loop(0, 4 * g.ny - 1)
    def _(slot):
        remote(block(zi), block(zi), pj_s.at[slot], pj_r.at[0], sibling).wait_send()

    @pl.loop(0, g.nt // 2)
    def _(n):
        rows = pl.ds(pl.multiple_of(n * 256, 256), 256)
        back = lax.dot_general(
            cot[...], full[rows, :], (((1,), (1,)), ((), ())), preferred_element_type=F32
        )
        dp[2 * n, HALO:HALO + g.f, :] = back[:, :LANES]
        dp[2 * n + 1, HALO:HALO + g.f, :] = back[:, LANES:]

    gathered(b1, 2, si, g.seq, in_seq)
    mean, squares = pooled(b1, g.seq, 16, sc[34])
    st1[0:g.nt, :] = mean
    st1[g.nt:2 * g.nt, :] = lax.rsqrt(squares * sc[34] + EPS)

    @pl.loop(0, g.nt)
    def _(l):
        lane = pl.ds(pl.multiple_of(l * LANES, LANES), LANES)
        mean_l = st1[pl.ds(l, 1), :]
        rstd_l = st1[pl.ds(g.nt + l, 1), :]
        gain_l = tap[l, g.k:g.k + 1, :]
        bias_l = tap[l, g.k + 1:g.k + 2, :]

        def step(r, sums):
            bias_sum, gain_sum = sums
            base = pl.multiple_of(r * g.chunk, g.chunk)
            rows = pl.ds(base + HALO, g.chunk)
            mask = keep[rows, :]
            normed = (cv[l, rows, :] - mean_l) * rstd_l
            cv[l, rows, :] = normed
            pre = normed * gain_l + bias_l
            sig = jax.nn.sigmoid(pre)
            hidden = mask * pre * sig
            hid[pl.ds(base, g.chunk), lane] = hidden.astype(BF16)
            hid_t[lane, pl.ds(base, g.chunk)] = hidden.T.astype(BF16)
            dpre = mask * dp[l, rows, :] * (sig * (1.0 + pre * (1.0 - sig)))
            dp[l, rows, :] = dpre
            return bias_sum + fold(dpre), gain_sum + fold(dpre * normed)

        zero = jnp.zeros((8, LANES), F32)
        bias_sum, gain_sum = lax.fori_loop(0, g.f // g.chunk, step, (zero, zero))
        a2[zi, pl.ds(l, 1), :] = jnp.sum(bias_sum, axis=0, keepdims=True)
        a2[zi, pl.ds(g.nt + l, 1), :] = jnp.sum(gain_sum, axis=0, keepdims=True)

    spread(a2, 3, zi, g.zero, in_zero)

    def hidden_rows(q, cc):
        return pl.ds(pl.multiple_of(zero_of(q % g.nzh, q // g.nzh, cc) * g.blk, 16), g.blk)

    def hidden_copy(q):
        return remote(
            hid_t.at[hidden_rows(q, 1 - c)],
            ht2.at[1, pl.ds(pl.multiple_of(q * g.blk, 16), g.blk)],
            ht_s.at[q], ht_r.at[q], sibling,
        )

    @pl.loop(0, g.q)
    def _(q):
        hidden_copy(q).start()

    edges = []
    for i, buf in enumerate((dp, cv)):
        edges.append(remote(
            buf.at[:, pl.ds(g.f, HALO), :], buf.at[:, pl.ds(0, HALO), :],
            hal2_s.at[2 * i], hal2_r.at[2 * i], right))
        edges.append(remote(
            buf.at[:, pl.ds(HALO, HALO), :], buf.at[:, pl.ds(g.f + HALO, HALO), :],
            hal2_s.at[2 * i + 1], hal2_r.at[2 * i + 1], left))
    for edge in edges:
        edge.start()

    @pl.loop(0, g.q)
    def _(q):
        ht2[0, pl.ds(pl.multiple_of(q * g.blk, 16), g.blk), :] = hid_t[hidden_rows(q, c), :]

    gathered(a2, 3, zi, g.zero, in_zero)
    total = a2[0]
    for i in range(1, g.zero):
        total = total + a2[i]
    b2[si] = total
    spread(b2, 4, si, g.seq, in_seq)

    cot_copy.wait()

    @pl.loop(0, g.q)
    def _(q):
        hidden_copy(q).wait()

    def part0_copy(o, target, sender):
        return remote(
            ws.at[0, :, :, target], r1x.at[sender], p1_s.at[0, o], p1_r.at[0, sender],
            in_seq(seq_of(target, zl)),
        )

    def part1_copy(o, target, sender):
        return remote(
            ws.at[1, target], r1y.at[sender], p1_s.at[1, o], p1_r.at[1, sender],
            in_zero(zero_of(zh, target, c)),
        )

    @pl.loop(1, g.nx + 1)
    def _(o):
        xx = (x + o) % g.nx
        col = pl.ds(pl.multiple_of(xx * g.cols, LANES), g.cols)
        wf[...] = jnp.dot(ht2[0], cot[:, col], preferred_element_type=F32) + jnp.dot(
            ht2[1], cot_sib[:, col], preferred_element_type=F32
        )
        for yy in range(g.ny):
            for hh in range(g.nzh):
                row = (yy * g.nzh + hh) * g.blk
                ws[0, yy, hh, xx] = wf[row:row + g.half, :].astype(BF16)
                ws[1, yy, hh, xx] = wf[row + g.half:row + g.blk, :].astype(BF16)
        for hh in range(g.nzh):
            row = pl.multiple_of((y * g.nzh + hh) * g.blk + g.half, 8)
            s1[hh, xx] = wf[pl.ds(row, g.half), :]

        @pl.when(o < g.nx)
        def _():
            part0_copy(o, xx, x).start()

    for yy in range(g.ny):
        for hh in range(g.nzh):
            row = (yy * g.nzh + hh) * g.blk
            s0[yy, hh] = wf[row:row + g.half, :]

    @pl.loop(1, g.ny)
    def _(o):
        part1_copy(o, (y + o) % g.ny, y).start()

    @pl.loop(0, g.nt // 2)
    def _(n):
        col = pl.ds(pl.multiple_of(n * 256, 256), 256)
        out[:, col] = jnp.dot(hid[...], full[:, col], preferred_element_type=F32).astype(BF16)

    gathered(b2, 4, si, g.seq, in_seq)
    total = b2[0]
    for i in range(1, g.seq):
        total = total + b2[i]
    st2[...] = total * sc[34]
    for edge in edges:
        edge.wait()

    def backward_tiles(first, last):
        @pl.loop(first, last)
        def _(l):
            lane = pl.ds(pl.multiple_of(l * LANES, LANES), LANES)
            scale = st1[pl.ds(g.nt + l, 1), :] * tap[l, g.k:g.k + 1, :]
            bias_m = st2[pl.ds(l, 1), :]
            gain_m = st2[pl.ds(g.nt + l, 1), :]
            dp[l] = keep[...] * scale * (dp[l] - bias_m - cv[l] * gain_m)
            gacc[...] = jnp.zeros(gacc.shape, F32)

            @pl.loop(0, g.f // g.chunk)
            def _(r):
                base = pl.multiple_of(r * g.chunk, g.chunk)
                here = dp[l, pl.ds(base + HALO, g.chunk), :]
                acc = jnp.zeros((g.chunk, LANES), F32)
                for k in range(g.k):
                    gacc[k] = gacc[k] + fold(here * x_s[l, pl.ds(base + k + 1, g.chunk), :])
                    acc = acc + tap[l, k:k + 1, :] * dp[l, pl.ds(base + 2 * HALO - 1 - k, g.chunk), :]
                mask = keep[pl.ds(base + HALO, g.chunk), :]
                gfeat[pl.ds(base, g.chunk), lane] = (mask * acc).astype(BF16)

            gfull[l, 0:32, :] = jnp.sum(gacc[...], axis=1)
            gfull[l, 32:g.krows, :] = jnp.zeros((g.krows - 32, LANES), F32)
            gfull[l, g.k:g.k + 1, :] = a2[zi, pl.ds(l, 1), :]
            gfull[l, g.k + 1:g.k + 2, :] = a2[zi, pl.ds(g.nt + l, 1), :]

    def second0_copy(o, target, sender):
        return remote(
            s0.at[target], r2y.at[sender], p2_s.at[0, o], p2_r.at[0, sender],
            in_zero(zero_of(zh, target, c)),
        )

    def second1_copy(o, target, sender):
        return remote(
            s1.at[:, target], r2x.at[sender], p2_s.at[1, o], p2_r.at[1, sender],
            in_seq(seq_of(target, zl)),
        )

    def third_copy(o):
        me = zh * g.nzl + zl
        peer = (me + o) % (g.nzh * g.nzl)
        hh, zz = peer // g.nzl, peer % g.nzl
        row = pl.ds(pl.multiple_of((zz % g.sub) * g.piece, 8), g.piece)
        return remote(
            tt.at[zz // g.sub, hh, row], r3.at[me], p3_s.at[o], p3_r.at[me],
            (zero_of(hh, y, c), seq_of(x, zz)),
        )

    def third_wait(o):
        me = zh * g.nzl + zl
        peer = (me + g.nzh * g.nzl - o) % (g.nzh * g.nzl)
        remote(r3.at[peer], r3.at[peer], p3_s.at[o], p3_r.at[peer], sibling).wait()

    backward_tiles(0, g.nt // 2)

    @pl.loop(1, g.nx)
    def _(o):
        part0_copy(o, x, (x + g.nx - o) % g.nx).wait()

    @pl.loop(1, g.ny)
    def _(o):
        part1_copy(o, y, (y + g.ny - o) % g.ny).wait()

    @pl.loop(1, g.nx)
    def _(o):
        s0[...] = s0[...] + r1x[(x + o) % g.nx].astype(F32)

    @pl.loop(1, g.ny)
    def _(o):
        s1[...] = s1[...] + r1y[(y + o) % g.ny].astype(F32)

    @pl.loop(1, g.ny)
    def _(o):
        second0_copy(o, (y + o) % g.ny, y).start()

    @pl.loop(1, g.nx)
    def _(o):
        second1_copy(o, (x + o) % g.nx, x).start()

    backward_tiles(g.nt // 2, g.nt)

    @pl.loop(1, g.ny)
    def _(o):
        second0_copy(o, y, (y + g.ny - o) % g.ny).wait()

    @pl.loop(1, g.nx)
    def _(o):
        second1_copy(o, x, (x + g.nx - o) % g.nx).wait()

    first = s0[y]
    second = s1[:, x]
    for o in range(1, g.ny):
        first = first + r2y[(y + o) % g.ny]
    for o in range(1, g.nx):
        second = second + r2x[(x + o) % g.nx]
    tt[0] = first
    tt[1] = second

    @pl.loop(1, g.nzh * g.nzl)
    def _(o):
        third_copy(o).start()

    lanes = lax.broadcasted_iota(jnp.int32, (g.krows, LANES), 1)
    for m in range(g.zero):
        t0, off = (m * g.blk) // LANES, (m * g.blk) % LANES
        value = gfull[t0]
        if off:
            value = pltpu.roll(value, LANES - off, 1)
            if off + g.blk > LANES:
                value = jnp.where(lanes < LANES - off, value, pltpu.roll(gfull[t0 + 1], LANES - off, 1))
        gsend[m] = value

    def owner_copy(o, target, sender):
        return remote(gsend.at[target], ga.at[sender], ssem.at[5, o], rsem.at[5, sender], in_zero(target))

    @pl.loop(1, g.zero)
    def _(o):
        owner_copy(o, (zi + o) % g.zero, zi).start()

    @pl.loop(1, g.nzh * g.nzl)
    def _(o):
        third_wait(o)

    mine = pl.ds(pl.multiple_of((zl % g.sub) * g.piece, 8), g.piece)
    r3[zh * g.nzl + zl] = tt[zl // g.sub, zh, mine, :]
    total = r3[0]
    for i in range(1, g.nzh * g.nzl):
        total = total + r3[i]
    if g.pad_piece > g.piece:
        total = jnp.concatenate([total, jnp.zeros((g.pad_piece - g.piece, g.cols), F32)], axis=0)
    wfin[si] = (total * sc[35]).astype(BF16)
    spread(wfin, 6, si, g.seq, in_seq)

    @pl.loop(1, g.zero)
    def _(o):
        owner_copy(o, zi, (zi + g.zero - o) % g.zero).wait()

    ga[zi] = gsend[zi]
    total = ga[0]
    for i in range(1, g.zero):
        total = total + ga[i]
    gb[si] = total
    spread(gb, 7, si, g.seq, in_seq)

    gathered(wfin, 6, si, g.seq, in_seq)
    for s in range(g.seq):
        row, col = (s % g.nzl) * g.piece, (s // g.nzl) * g.cols
        asm[row:row + g.piece, col:col + g.cols] = wfin[s].astype(F32)[0:g.piece]
    gproj[...] = asm[...].astype(BF16)

    gathered(gb, 7, si, g.seq, in_seq)
    total = gb[0]
    for i in range(1, g.seq):
        total = total + gb[i]
    gsmall[...] = total * sc[35]


def fused(g, *operands):
    vmem = pltpu.VMEM
    dma = pltpu.SemaphoreType.DMA
    planes = (g.nt, g.ext, LANES)
    stats = (2 * g.nt, LANES)
    scratch = [
        vmem(planes, F32),
        vmem(planes, F32),
        vmem(planes, F32),
        vmem((g.nt, g.srows, LANES), F32),
        vmem((g.d, g.d), BF16),
        vmem((g.f, g.d), BF16),
        vmem((g.d, g.f), BF16),
        vmem((2, g.q * g.blk, g.f), BF16),
        vmem((g.f, g.d), BF16),
        vmem((2, HALO, g.d), BF16),
        vmem((g.zero, g.srows, LANES), BF16),
        vmem((g.zero,) + stats, F32),
        vmem((g.seq,) + stats, F32),
        vmem((g.zero,) + stats, F32),
        vmem((g.seq,) + stats, F32),
        vmem(stats, F32),
        vmem(stats, F32),
        vmem((32, 8, LANES), F32),
        vmem((g.nt, g.krows, LANES), F32),
        vmem((g.zero, g.krows, LANES), F32),
        vmem((g.zero, g.krows, LANES), F32),
        vmem((g.seq, g.krows, LANES), F32),
        vmem((g.q * g.blk, g.cols), F32),
        vmem((2, g.ny, g.nzh, g.nx, g.half, g.cols), BF16),
        vmem((g.nx, g.ny, g.nzh, g.half, g.cols), BF16),
        vmem((g.ny, g.nzh, g.nx, g.half, g.cols), BF16),
        vmem((g.ny, g.nzh, g.half, g.cols), F32),
        vmem((g.nzh, g.nx, g.half, g.cols), F32),
        vmem((g.nx, g.nzh, g.half, g.cols), F32),
        vmem((g.ny, g.nzh, g.half, g.cols), F32),
        vmem((2, g.nzh, g.half, g.cols), F32),
        vmem((g.nzh * g.nzl, g.piece, g.cols), F32),
        vmem((g.seq, g.pad_piece, g.cols), BF16),
        vmem((g.blk, g.d), F32),
        dma((8, 16)), dma((8, 16)),
        dma((2,)), dma((2,)), dma((4,)), dma((4,)), dma, dma,
        dma((4 * g.ny,)), dma((g.zero,)), dma((g.q,)), dma((g.q,)),
        dma((2, 4)), dma((2, 4)), dma((2, 4)), dma((2, 4)),
        dma((g.nzh * g.nzl,)), dma((g.nzh * g.nzl,)),
    ]
    whole = pl.BlockSpec(memory_space=pltpu.VMEM)
    return pl.pallas_call(
        functools.partial(kernel, g),
        name="conformer_conv",
        out_shape=[
            jax.ShapeDtypeStruct((g.f, g.d), BF16),
            jax.ShapeDtypeStruct((g.f, g.d), BF16),
            jax.ShapeDtypeStruct((g.blk, g.d), BF16),
            jax.ShapeDtypeStruct((g.krows, LANES), F32),
        ],
        in_specs=[pl.BlockSpec(memory_space=pltpu.SMEM)] + [whole] * 5,
        out_specs=[whole] * 4,
        scratch_shapes=scratch,
        compiler_params=pltpu.CompilerParams(
            collective_id=0, has_side_effects=True, vmem_limit_bytes=56 * 1024 * 1024
        ),
    )(*operands)


def shards(features, lengths, kernel_taps, gain, bias, projection, cotangent):
    frames, width = features.shape[1:]
    taps = kernel_taps.shape[0]
    zero, seq = lax.axis_size("zero"), lax.axis_size("seq")
    g = Dims(zero, seq, frames, width, taps)
    member, place = lax.axis_index("zero"), lax.axis_index("seq")
    here = place * frames
    own_length = lengths[member]
    positions = here - HALO + jnp.arange(g.ext, dtype=jnp.int32)
    keep = ((positions >= 0) & (positions < own_length)).astype(F32)
    keep = jnp.broadcast_to(keep[:, None], (g.ext, LANES))
    spans = jnp.clip(lengths[:, None] - jnp.arange(seq, dtype=jnp.int32)[None, :] * frames, 0, frames)
    valid_a = lax.dynamic_index_in_dim(spans, place, axis=1, keepdims=False).astype(F32)
    valid_b = jnp.sum(spans, axis=0).astype(F32)
    count = jnp.sum(lengths).astype(F32)

    def inverse(n):
        return 1.0 / jnp.maximum(n, 1.0)

    scalars = jnp.concatenate([
        jnp.pad(valid_a, (0, 16 - zero)), jnp.pad(valid_b, (0, 16 - seq)),
        jnp.stack([
            inverse(valid_a[member]), inverse(valid_b[place]), 1.0 / count, lax.rsqrt(count),
        ]),
    ])
    small = jnp.concatenate([kernel_taps, gain[None, :], bias[None, :]], axis=0)
    small = jnp.pad(small, ((0, g.srows - small.shape[0]), (0, LANES - small.shape[1])))
    out, gfeat, gproj, gsmall = fused(
        g, scalars, features[0], cotangent[0], projection, small, keep
    )
    return (
        out[None], gfeat[None], gproj,
        gsmall[:taps, :g.blk].astype(BF16),
        gsmall[taps + 1, :g.blk],
        gsmall[taps, :g.blk],
    )


def solution(mesh):
    in_specs = (
        P("zero", "seq", None),
        P(),
        P(None, "zero"),
        P("zero"),
        P("zero"),
        P("zero", None),
        P("zero", "seq", None),
    )
    out_specs = (
        P("zero", "seq", None),
        P("zero", "seq", None),
        P("zero", None),
        P(None, "zero"),
        P("zero"),
        P("zero"),
    )
    return jax.shard_map(shards, mesh=mesh, in_specs=in_specs, out_specs=out_specs, check_vma=False)
```

time: 633 us -> 155 us (0.24); the launches traced: 622 us -> 155 us
  blocking collectives: 360 us -> 0 us
  Pallas kernels: 0 us -> 137 us
  other arithmetic: 108 us -> 4.75 us
  waiting for transfers between devices: 99.7 us -> 0 us
  matrix products: 23.8 us -> 0 us
  between operations: 15 us -> 2.8 us
  starting transfers between devices: 11.1 us -> 0 us
  local copies, waits for them, and re-layouts: 3.96 us -> 10.4 us
    psum x4 -> x0, blocking collectives: 326 us -> none  [the longest x1 107 us: shards(): lax.psum((jnp.sum(dpre, axis=0), jnp.sum(dpre * normed, axis=0)), ('zero'...]
    pallas_call x0 -> x1, Pallas kernels: none -> 137 us  [fused(): pl.pallas_call(functools.partial(kernel, g), name='conformer_conv', out_s...]
    psum x1 -> x0, waiting for transfers between devices: 85.3 us -> none  [shards(): weight_total, kernel_total = lax.psum((weight_part, kernel_part), 'seq')]
    broadcast_in_dim x1 -> x0, other arithmetic: 51 us -> none  [shards(): grad_features = (keep * dframes).astype(jnp.bfloat16)[None]]
    reduce_sum x5 -> x2, other arithmetic: 50.2 us -> 2.13 us  [the longest x1 1.29 us: shards(): count = jnp.sum(lengths).astype(F32)]
    all_gather x1 -> x0, blocking collectives: 34.1 us -> none  [shards(): lax.all_gather(small, 'zero', axis=1, tiled=True)]
    dot_general x3 -> x0, matrix products: 23.8 us -> none  [the longest x1 8.64 us: shards(): lax.dot_general(hidden, upstream, (((0,), (0,)), ((), ())), preferred_ele...]
    unnamed x5 -> x0, waiting for transfers between devices: 14.4 us -> none
  transfers between devices with their start and end apart: 8 -> 0, of which waited for: 2 -> 0; matrix products, arithmetic and copies ran while one was open for 22% -> 0% of each run, Pallas kernels for 0% -> 0%
where the time goes in v1:
time: 155 us
  Pallas kernels  137 us (88%)
  local copies, waits for them, and re-layouts  10.4 us (7%)
  other arithmetic  4.75 us (3%)
  between operations  2.8 us (2%)
    pallas_call x1, Pallas kernels, fused(): pl.pallas_call(functools.partial(kernel, g), name='conformer_conv', out_s...  137 us
    unnamed x7, local copies, waits for them, and re-layouts  4.63 us

profile of v1, /device:TPU:1, one launch (start us, length us, event | category | flops | bytes accessed | tf_op | source)
XLA Modules:
  0.0 155.0 jit_solution(12359281260984825882)
XLA Ops:
  0.6 1.2 dynamic_slice.16
  1.9 1.3 reduce_sum.19
  3.9 0.7 fusion.12
  4.6 0.8 fusion.13
  5.4 0.6 dynamic_slice.15
  6.7 0.6 fusion.14
  8.0 0.6 concatenate.6.sc
  8.6 1.3 fusion.8.small
  10.0 0.8 broadcast_in_dim.22.keep
  10.8 137.0 %conformer_conv.1 = (bf16[512,1536]{1,0:T(8,128)(2,1)}, bf16[512,1536]{1,0:T(8,128)(2,1)}, bf16[96,1536]{1,0:T(8,128)(2,1)}, f32[40,128]{1,0:T(8,128)}) custom-call(f32[36]{0:T(128)} %concatenate.6.sc, bf16[512,1536]{1,0:T(8,128)(2,1)} %bitcast.16, bf16[512,1536]{1,0:T(8,128)(2,1)} %bitcast.17, bf16[96,1536]{1,0:T(8,128)(2,1)} %proj.1, ...), custom_call_target="tpu_custom_call" | custom-call | tf_op jit(solution)/shard_map/conformer_conv/pallas_call | solution.py:581
  147.9 1.2 slice_bitcast_fusion
  149.1 1.3 slice.17
  150.4 0.0 copy-start
  150.4 2.8 %copy.16 = bf16[1,512,1536]{2,1,0:T(8,128)(2,1)} copy(bf16[1,512,1536]{2,1,0:T(8,128)(2,1)} %bitcast.19) | data formatting | bytes 3145728
  153.1 0.0 copy-done
  153.1 0.0 copy-start.1
  153.2 1.1 copy.17
  154.3 0.0 copy-done.1
  154.3 0.7 copy.18
  (4 shorter events, 0.0 us)
Async XLA Ops:
  150.4 2.8 %copy-start = (bf16[512,1536]{1,0:T(8,128)(2,1)S(1)}, bf16[512,1536]{1,0:T(8,128)(2,1)}, u32[]{:S(2)}) copy-start(bf16[512,1536]{1,0:T(8,128)(2,1)} %get-tuple-element.11) | copy-start | bytes 4718596
  153.1 1.1 copy-start.1
